TPU v7x, 32 devices: a whole 2x2x4 slice. The times are simulated.
32 devices in a mesh: col: 4 (over y, x), ta: 8 (over z, core).
Axes of the slice: x: 2, y: 2, z: 4, core: 2. Of those that a mesh axis runs over, the one named last changes fastest.
Arguments:
- frames: bfloat16 [672, 14, 14, 1024], P(('col', 'ta')), may hold values from -6 to 6
- out_grad: bfloat16 [672, 14, 14, 1024], P(('col', 'ta')), may hold values from -6 to 6
- held: int32 [4, 8], replicated, may hold values from 3 to 21, as said below
- clip_stride: int32 [4, 24], replicated, may hold values from 1 to 4, as said below
- w_reduce: bfloat16 [2, 1024, 256], replicated, may hold values from -0.1875 to 0.1875
- w_mid: bfloat16 [2, 256, 256], replicated, may hold values from -0.375 to 0.375
- depth_kernel: bfloat16 [2, 27, 256], replicated, may hold values from -1.25 to 1.25
- w_expand: bfloat16 [2, 256, 1024], replicated, may hold values from -0.375 to 0.375
- narrow_gain: bfloat16 [2, 2, 256], replicated, may hold values from 0.099609375 to 1.8984375
- narrow_bias: bfloat16 [2, 2, 256], replicated, may hold values from -3 to 3
- wide_gain: bfloat16 [2, 1024], replicated, may hold values from 0.099609375 to 1.8984375
- wide_bias: bfloat16 [2, 1024], replicated, may hold values from -3 to 3
Outputs:
- block_output: bfloat16 [672, 14, 14, 1024], P(('col', 'ta'))
- grad_frames: bfloat16 [672, 14, 14, 1024], P(('col', 'ta'))
- grad_w_reduce: float32 [2, 1024, 256], replicated
- grad_w_mid: float32 [2, 256, 256], replicated
- grad_depth_kernel: float32 [2, 27, 256], replicated
- grad_w_expand: float32 [2, 256, 1024], replicated
- grad_narrow_gain: float32 [2, 2, 256], replicated
- grad_narrow_bias: float32 [2, 2, 256], replicated
- grad_wide_gain: float32 [2, 1024], replicated
- grad_wide_bias: float32 [2, 1024], replicated
Inputs may be any that keep to these rules, and one draw needn't show every extreme that they name: `held`: devices 2i and 2i + 1 of ta hold 24 live frames together, in every clip group. `clip_stride`: in each group a quarter of the clips have stride 1 (8 frames), a quarter stride 2 (4 frames) and half stride 4 (2 frames), in any order.
All inputs are finite; a program needn't handle non-finite values.
Results may differ from a plain program's by a relative error of at most 0.017.
Values may be sent and summed in bfloat16 or wider, within the bound.
A program may use at most 320 MiB of HBM per device.

v0:
```python
import jax
import jax.numpy as jnp
from jax import lax
from jax.sharding import PartitionSpec as P

FR_DEV = 12
EPS = 1e-05


def extended(shard, sides, width):
    for axis, dim in sides:
        devices, length = (lax.axis_size(axis), shard.shape[dim])
        up = [(i, (i + 1) % devices) for i in range(devices - 1)]
        down = [(j, i) for i, j in up]
        last = lax.slice_in_dim(shard, length - width, length, axis=dim)
        first = lax.slice_in_dim(shard, 0, width, axis=dim)
        before = lax.ppermute(last, axis, up)
        after = lax.ppermute(first, axis, down)
        shard = jnp.concatenate([before, shard, after], axis=dim)
    return shard


def silu_slope(values):
    sigmoid_v = jax.nn.sigmoid(values)
    return sigmoid_v * (1.0 + values * (1.0 - sigmoid_v))


def normalize(values, alive_rows, summed_count, gain_vec, bias_vec):
    average = lax.psum(jnp.sum(values * alive_rows, axis=0), ("col", "ta")) / summed_count
    centred = values - average
    spread = lax.psum(jnp.sum(centred * centred * alive_rows, axis=0), ("col", "ta")) / summed_count
    inverse = lax.rsqrt(spread + EPS)
    normed = (values - average) * inverse
    return (normed, inverse, gain_vec * normed + bias_vec)


def normalize_back(grad_z, normed, inverse, gain_vec, alive_rows, summed_count):
    grad_bias, grad_gain = lax.psum(
        (jnp.sum(grad_z, axis=0), jnp.sum(grad_z * normed, axis=0)), ("col", "ta")
    )
    grad_input = (
        gain_vec * inverse * (grad_z - grad_bias / summed_count - normed * grad_gain / summed_count)
    )
    return (grad_input * alive_rows, grad_gain, grad_bias)


def padded_planes(source):
    return jnp.pad(source, ((0, 0), (1, 1), (1, 1), (0, 0)))


def spatial_apply(source, kernel, plane_id):
    padded = padded_planes(source)
    span_h, span_w = (source.shape[1], source.shape[2])
    result = jnp.zeros(source.shape, jnp.float32)
    for row_off in range(3):
        for col_off in range(3):
            result = (
                result
                + kernel[plane_id * 9 + row_off * 3 + col_off]
                * padded[:, row_off : row_off + span_h, col_off : col_off + span_w, :]
            )
    return result


def spatial_transpose(grid_grad, kernel, plane_id):
    padded = padded_planes(grid_grad)
    span_h, span_w = (grid_grad.shape[1], grid_grad.shape[2])
    result = jnp.zeros(grid_grad.shape, jnp.float32)
    for row_off in range(3):
        for col_off in range(3):
            result = (
                result
                + kernel[plane_id * 9 + row_off * 3 + col_off]
                * padded[
                    :, 2 - row_off : 2 - row_off + span_h, 2 - col_off : 2 - col_off + span_w, :
                ]
            )
    return result


def spatial_kernel_grad(grid_grad, source):
    padded = padded_planes(source)
    span_h, span_w = (source.shape[1], source.shape[2])
    rows_out = []
    for row_off in range(3):
        for col_off in range(3):
            rows_out.append(
                jnp.sum(
                    grid_grad
                    * padded[:, row_off : row_off + span_h, col_off : col_off + span_w, :],
                    axis=(0, 1, 2),
                )
            )
    return jnp.stack(rows_out)


def add_at(target, addend, position):
    current = lax.dynamic_slice_in_dim(target, position, 1, 0)
    return lax.dynamic_update_slice_in_dim(target, current + addend, position, 0)


def neighbour_masks(stride_row, first_frame, slots, count, frames_total):
    lengths = 8 // stride_row
    starts = jnp.cumsum(lengths) - lengths
    global_ids = first_frame + jnp.arange(slots)
    begins = jnp.sum((starts[None, :] == global_ids[:, None]).astype(jnp.int32), axis=1) > 0
    following = jnp.sum((starts[None, :] == global_ids[:, None] + 1).astype(jnp.int32), axis=1) > 0
    alive = jnp.arange(slots) < count
    prev_ok = alive & jnp.logical_not(begins)
    next_ok = alive & jnp.logical_not(following) & (global_ids + 1 < frames_total)
    return (alive, prev_ok, next_ok)


def body(
    frames,
    out_grad,
    held,
    clip_stride,
    w_reduce,
    w_mid,
    depth_kernel,
    w_expand,
    narrow_gain,
    narrow_bias,
    wide_gain,
    wide_bias,
):
    col_pos = lax.axis_index("col")
    ta_pos = lax.axis_index("ta")
    held_row = jnp.take(held, col_pos, axis=0)
    held_here = jnp.take(held_row, ta_pos)
    capacity, span_h, span_w, width = frames.shape
    pixels = span_h * span_w
    frames_total = held.shape[1] * FR_DEV
    summed_count = float(held.shape[0] * frames_total * pixels)
    arrival_alive = jnp.arange(capacity) < held_here
    grad_in = jnp.where(arrival_alive[:, None, None, None], out_grad, jnp.zeros((), out_grad.dtype))
    first_frame = jnp.sum(jnp.where(jnp.arange(held_row.shape[0]) < ta_pos, held_row, 0))
    slots = frames.shape[0]
    alive, prev_ok, next_ok = neighbour_masks(
        jnp.take(clip_stride, col_pos, axis=0), first_frame, slots, held_here, frames_total
    )
    alive_rows = jnp.repeat(alive.astype(jnp.float32), pixels)[:, None]
    alive_grid = alive.astype(jnp.float32)[:, None, None, None]
    prev_grid = prev_ok.astype(jnp.float32)[:, None, None, None]
    next_grid = next_ok.astype(jnp.float32)[:, None, None, None]
    bottleneck = w_mid.shape[1]
    zero_frame = jnp.zeros((1, span_h, span_w, bottleneck), jnp.bfloat16)
    act_low = frames.reshape(-1, width)
    act_full = act_low.astype(jnp.float32)
    saved = []
    for block_id in range(w_reduce.shape[0]):
        gains_narrow = narrow_gain[block_id].astype(jnp.float32)
        biases_narrow = narrow_bias[block_id].astype(jnp.float32)
        h_one = jnp.dot(act_low, w_reduce[block_id], preferred_element_type=jnp.float32)
        normed_one, inverse_one, z_one = normalize(
            h_one, alive_rows, summed_count, gains_narrow[0], biases_narrow[0]
        )
        u_one_low = jax.nn.silu(z_one).astype(jnp.bfloat16)
        h_two = jnp.dot(u_one_low, w_mid[block_id], preferred_element_type=jnp.float32).astype(
            jnp.bfloat16
        )
        grid = h_two.reshape(slots, span_h, span_w, bottleneck)
        rims = jnp.stack(
            [grid[0], lax.dynamic_index_in_dim(grid, held_here - 1, 0, keepdims=False)]
        )
        outer = extended(rims, (("ta", 0),), 1)
        earlier = jnp.concatenate([outer[0:1], grid[:-1]]).astype(jnp.float32) * prev_grid
        later_base = lax.dynamic_update_slice_in_dim(
            jnp.concatenate([grid[1:], zero_frame]), outer[3:4], held_here - 1, 0
        )
        later = later_base.astype(jnp.float32) * next_grid
        kernel = depth_kernel[block_id].astype(jnp.float32)
        sources = (earlier, grid.astype(jnp.float32), later)
        depth = (
            spatial_apply(sources[0], kernel, 0)
            + spatial_apply(sources[1], kernel, 1)
            + spatial_apply(sources[2], kernel, 2)
        )
        normed_two, inverse_two, z_two = normalize(
            depth.reshape(-1, bottleneck),
            alive_rows,
            summed_count,
            gains_narrow[1],
            biases_narrow[1],
        )
        u_two_low = jax.nn.silu(z_two).astype(jnp.bfloat16)
        h_three = jnp.dot(u_two_low, w_expand[block_id], preferred_element_type=jnp.float32)
        normed_three, inverse_three, z_three = normalize(
            h_three,
            alive_rows,
            summed_count,
            wide_gain[block_id].astype(jnp.float32),
            wide_bias[block_id].astype(jnp.float32),
        )
        pre_act = act_full + z_three
        saved.append(
            (
                act_low,
                normed_one,
                inverse_one,
                z_one,
                u_one_low,
                sources,
                normed_two,
                inverse_two,
                z_two,
                u_two_low,
                normed_three,
                inverse_three,
                pre_act,
            )
        )
        act_full = jax.nn.silu(pre_act)
        act_low = act_full.astype(jnp.bfloat16)
    grad_out = grad_in.reshape(-1, width).astype(jnp.float32)
    grads_reduce, grads_mid, grads_kernel, grads_expand = ([], [], [], [])
    grads_ngain, grads_nbias, grads_wgain, grads_wbias = ([], [], [], [])
    for block_id in reversed(range(w_reduce.shape[0])):
        (
            block_low,
            normed_one,
            inverse_one,
            z_one,
            u_one_low,
            sources,
            normed_two,
            inverse_two,
            z_two,
            u_two_low,
            normed_three,
            inverse_three,
            pre_act,
        ) = saved[block_id]
        gains_narrow = narrow_gain[block_id].astype(jnp.float32)
        kernel = depth_kernel[block_id].astype(jnp.float32)
        grad_pre = grad_out * silu_slope(pre_act)
        grad_h3, gain_three, bias_three = normalize_back(
            grad_pre,
            normed_three,
            inverse_three,
            wide_gain[block_id].astype(jnp.float32),
            alive_rows,
            summed_count,
        )
        grad_h3_low = grad_h3.astype(jnp.bfloat16)
        grads_expand.append(
            jnp.einsum("vc,vd->cd", u_two_low, grad_h3_low, preferred_element_type=jnp.float32)
        )
        grad_u2 = jnp.einsum(
            "vd,cd->vc", grad_h3_low, w_expand[block_id], preferred_element_type=jnp.float32
        )
        grad_depth, gain_two, bias_two = normalize_back(
            grad_u2 * silu_slope(z_two),
            normed_two,
            inverse_two,
            gains_narrow[1],
            alive_rows,
            summed_count,
        )
        grid_grad = grad_depth.reshape(slots, span_h, span_w, bottleneck)
        grads_kernel.append(
            jnp.concatenate(
                [
                    spatial_kernel_grad(grid_grad, sources[0]),
                    spatial_kernel_grad(grid_grad, sources[1]),
                    spatial_kernel_grad(grid_grad, sources[2]),
                ]
            )
        )
        toward_prev = spatial_transpose(grid_grad, kernel, 0) * prev_grid
        toward_self = spatial_transpose(grid_grad, kernel, 1)
        toward_next = spatial_transpose(grid_grad, kernel, 2) * next_grid
        rims_back = jnp.stack(
            [
                toward_prev[0],
                lax.dynamic_index_in_dim(toward_next, held_here - 1, 0, keepdims=False),
            ]
        )
        outer_back = extended(rims_back.astype(jnp.bfloat16), (("ta", 0),), 1).astype(
            rims_back.dtype
        )
        zero_grad = jnp.zeros((1, span_h, span_w, bottleneck), jnp.float32)
        from_later = add_at(
            jnp.concatenate([toward_prev[1:], zero_grad]), outer_back[3:4], held_here - 1
        )
        from_earlier = add_at(jnp.concatenate([zero_grad, toward_next[:-1]]), outer_back[0:1], 0)
        grad_h2 = (
            ((toward_self + from_later + from_earlier) * alive_grid)
            .reshape(-1, bottleneck)
            .astype(jnp.bfloat16)
        )
        grads_mid.append(
            jnp.einsum("vc,vd->cd", u_one_low, grad_h2, preferred_element_type=jnp.float32)
        )
        grad_u1 = jnp.einsum(
            "vd,cd->vc", grad_h2, w_mid[block_id], preferred_element_type=jnp.float32
        )
        grad_h1, gain_one, bias_one = normalize_back(
            grad_u1 * silu_slope(z_one),
            normed_one,
            inverse_one,
            gains_narrow[0],
            alive_rows,
            summed_count,
        )
        grad_h1_low = grad_h1.astype(jnp.bfloat16)
        grads_reduce.append(
            jnp.einsum("vc,vd->cd", block_low, grad_h1_low, preferred_element_type=jnp.float32)
        )
        grad_out = (
            jnp.einsum(
                "vb,db->vd", grad_h1_low, w_reduce[block_id], preferred_element_type=jnp.float32
            )
            + grad_pre
        )
        grads_ngain.append(jnp.stack([gain_one, gain_two]))
        grads_nbias.append(jnp.stack([bias_one, bias_two]))
        grads_wgain.append(gain_three)
        grads_wbias.append(bias_three)
    out_low = act_full.reshape(slots, span_h, span_w, width).astype(jnp.bfloat16)
    grad_low = grad_out.reshape(slots, span_h, span_w, width).astype(jnp.bfloat16)
    block_output = jnp.where(
        arrival_alive[:, None, None, None], out_low, jnp.zeros((), jnp.bfloat16)
    )
    grad_frames = jnp.where(
        arrival_alive[:, None, None, None], grad_low, jnp.zeros((), jnp.bfloat16)
    )
    summed_reduce, summed_mid, summed_kernel, summed_expand = lax.psum(
        (
            jnp.stack(grads_reduce[::-1]),
            jnp.stack(grads_mid[::-1]),
            jnp.stack(grads_kernel[::-1]),
            jnp.stack(grads_expand[::-1]),
        ),
        ("col", "ta"),
    )
    return (
        block_output,
        grad_frames,
        summed_reduce,
        summed_mid,
        summed_kernel,
        summed_expand,
        jnp.stack(grads_ngain[::-1]),
        jnp.stack(grads_nbias[::-1]),
        jnp.stack(grads_wgain[::-1]),
        jnp.stack(grads_wbias[::-1]),
    )


def solution(mesh):
    placed = (
        P(("col", "ta"), None, None, None),
        P(("col", "ta"), None, None, None),
        P(),
        P(),
        P(),
        P(),
        P(),
        P(),
        P(),
        P(),
        P(),
        P(),
    )
    return jax.shard_map(
        body,
        mesh=mesh,
        in_specs=placed,
        out_specs=(
            P(("col", "ta"), None, None, None),
            P(("col", "ta"), None, None, None),
            P(),
            P(),
            P(),
            P(),
            P(),
            P(),
            P(),
            P(),
        ),
        check_vma=False,
    )
```

profile of v0, /device:TPU:0, one launch (start us, length us, event | category | flops | bytes accessed | tf_op | source)
XLA Modules:
  0.0 1641.1 jit_solution(1639509669055725143)
XLA Ops:
  10.0 12.9 reshape.475
  22.9 7.9 multiply_reduce_fusion.71
  30.7 42.0 %psum.196 = f32[256]{0:T(256)S(1)} all-reduce(f32[256]{0:T(256)S(1)} %get-tuple-element.276), channel_id=1, replica_groups=mesh['col'=4,'ta'=8] {'col','ta'}, use_global_device_ids=true, to_apply=%region_1.2 | all-reduce | flops 256 | bytes 2048 | tf_op jit(solution)/shard_map/psum | solution.py:29
  76.1 40.2 %psum.197 = f32[256]{0:T(256)S(1)} all-reduce(f32[256]{0:T(256)S(1)} %multiply_reduce_fusion.70), channel_id=1, replica_groups=mesh['col'=4,'ta'=8] {'col','ta'}, use_global_device_ids=true, to_apply=%region_3.4 | all-reduce | flops 256 | bytes 2048 | tf_op jit(solution)/shard_map/psum | solution.py:31
  135.0 11.8 select_convert_fusion
  157.6 18.5 %reshape.564 = f32[4116,1024]{1,0:T(8,128)} reshape(f32[21,14,14,1024]{3,2,1,0:T(8,128)} %select_convert_fusion) | data formatting | bytes 33718272 | tf_op jit(solution)/shard_map/convert_element_type | solution.py:216
  185.2 60.1 %multiply_reduce_fusion.59 = (f32[256]{0:T(256)S(1)}, f32[21,14,14,256]{3,2,1,0:T(8,128)}) fusion(f32[21]{0:T(128)S(1)} %fusion.67, f32[256]{0:T(256)S(1)} %bitcast.279, f32[256]{0:T(256)S(1)} %bitcast.281, f32[256]{0:T(256)S(1)} %bitcast.283, f32[256]{0:T(256)S(1)} %bitcast.285, f32[21,14,14,256]{3,2,1,0:T(8,128)} %convert_multiply_fusion.1, ...), kind=kLoop, calls=%fused_computation.159 | loop fusion | flops 57953024 | bytes 16887892 | tf_op jit(solution)/shard_map/reduce_sum | solution.py:29
  245.4 43.0 %psum.198 = f32[256]{0:T(256)S(1)} all-reduce(f32[256]{0:T(256)S(1)} %get-tuple-element.178), channel_id=1, replica_groups=mesh['col'=4,'ta'=8] {'col','ta'}, use_global_device_ids=true, to_apply=%region_9.10 | all-reduce | flops 256 | bytes 2048 | tf_op jit(solution)/shard_map/psum | solution.py:29
  291.7 40.4 %psum.199 = f32[256]{0:T(256)S(1)} all-reduce(f32[256]{0:T(256)S(1)} %multiply_reduce_fusion.58), channel_id=1, replica_groups=mesh['col'=4,'ta'=8] {'col','ta'}, use_global_device_ids=true, to_apply=%region_11.12 | all-reduce | flops 256 | bytes 2048 | tf_op jit(solution)/shard_map/psum | solution.py:31
  338.5 9.8 multiply_reduce_fusion.5
  348.3 40.1 %psum.200 = f32[1024]{0:T(1024)S(1)} all-reduce(f32[1024]{0:T(1024)S(1)} %get-tuple-element.278), channel_id=1, replica_groups=mesh['col'=4,'ta'=8] {'col','ta'}, use_global_device_ids=true, to_apply=%region_13.14 | all-reduce | flops 1024 | bytes 8192 | tf_op jit(solution)/shard_map/psum | solution.py:29
  388.3 7.3 multiply_reduce_fusion.4
  395.6 40.0 %psum.201 = f32[1024]{0:T(1024)S(1)} all-reduce(f32[1024]{0:T(1024)S(1)} %multiply_reduce_fusion.4), channel_id=1, replica_groups=mesh['col'=4,'ta'=8] {'col','ta'}, use_global_device_ids=true, to_apply=%region_15.16 | all-reduce | flops 1024 | bytes 8192 | tf_op jit(solution)/shard_map/psum | solution.py:31
  436.3 10.9 fusion
  454.2 40.2 %psum.202 = f32[256]{0:T(256)S(1)} all-reduce(f32[256]{0:T(256)S(1)} %get-tuple-element.280), channel_id=1, replica_groups=mesh['col'=4,'ta'=8] {'col','ta'}, use_global_device_ids=true, to_apply=%region_17.18 | all-reduce | flops 256 | bytes 2048 | tf_op jit(solution)/shard_map/psum | solution.py:29
  497.8 40.0 %psum.203 = f32[256]{0:T(256)S(1)} all-reduce(f32[256]{0:T(256)S(1)} %multiply_reduce_fusion.68), channel_id=1, replica_groups=mesh['col'=4,'ta'=8] {'col','ta'}, use_global_device_ids=true, to_apply=%region_19.20 | all-reduce | flops 256 | bytes 2048 | tf_op jit(solution)/shard_map/psum | solution.py:31
  587.2 59.2 %multiply_reduce_fusion.57 = (f32[256]{0:T(256)S(1)}, f32[21,14,14,256]{3,2,1,0:T(8,128)}) fusion(f32[21]{0:T(128)S(1)} %fusion.67, f32[256]{0:T(256)S(1)} %bitcast.349, f32[256]{0:T(256)S(1)} %bitcast.351, f32[256]{0:T(256)S(1)} %bitcast.353, f32[256]{0:T(256)S(1)} %bitcast.355, f32[21,14,14,256]{3,2,1,0:T(8,128)} %convert_multiply_fusion, ...), kind=kLoop, calls=%fused_computation.154 | loop fusion | flops 57953024 | bytes 16887892 | tf_op jit(solution)/shard_map/reduce_sum | solution.py:29
  646.4 43.3 %psum.204 = f32[256]{0:T(256)S(1)} all-reduce(f32[256]{0:T(256)S(1)} %get-tuple-element.176), channel_id=1, replica_groups=mesh['col'=4,'ta'=8] {'col','ta'}, use_global_device_ids=true, to_apply=%region_21.22 | all-reduce | flops 256 | bytes 2048 | tf_op jit(solution)/shard_map/psum | solution.py:29
  698.4 40.0 %psum.205 = f32[256]{0:T(256)S(1)} all-reduce(f32[256]{0:T(256)S(1)} %multiply_reduce_fusion.56), channel_id=1, replica_groups=mesh['col'=4,'ta'=8] {'col','ta'}, use_global_device_ids=true, to_apply=%region_23.24 | all-reduce | flops 256 | bytes 2048 | tf_op jit(solution)/shard_map/psum | solution.py:31
  744.2 9.8 multiply_reduce_fusion.3
  754.0 40.1 %psum.206 = f32[1024]{0:T(1024)S(1)} all-reduce(f32[1024]{0:T(1024)S(1)} %get-tuple-element.282), channel_id=1, replica_groups=mesh['col'=4,'ta'=8] {'col','ta'}, use_global_device_ids=true, to_apply=%region_25.26 | all-reduce | flops 1024 | bytes 8192 | tf_op jit(solution)/shard_map/psum | solution.py:29
  794.0 7.3 multiply_reduce_fusion.2
  801.3 40.4 %psum.207 = f32[1024]{0:T(1024)S(1)} all-reduce(f32[1024]{0:T(1024)S(1)} %multiply_reduce_fusion.2), channel_id=1, replica_groups=mesh['col'=4,'ta'=8] {'col','ta'}, use_global_device_ids=true, to_apply=%region_27.28 | all-reduce | flops 1024 | bytes 8192 | tf_op jit(solution)/shard_map/psum | solution.py:31
  841.8 25.8 %fusion.69 = (f32[1024]{0:T(1024)S(1)}, f32[1024]{0:T(1024)S(1)}, f32[4116,1024]{1,0:T(8,128)}, bf16[4116,1024]{1,0:T(8,128)(2,1)}) fusion(f32[1024]{0:T(1024)S(1)} %get-tuple-element.249, f32[4116,1024]{1,0:T(8,128)} %get-tuple-element.283, f32[1024]{0:T(1024)S(1)} %broadcast_multiply_fusion.4, f32[4116,1024]{1,0:T(8,128)} %reshape.564, ...), kind=kLoop, calls=%fused_computation.336 | loop fusion | flops 75864064 | bytes 75890688 | tf_op jit(solution)/shard_map/reduce_sum | solution.py:39
  867.6 40.1 %all-reduce.17 = (f32[1024]{0:T(1024)S(1)}, f32[1024]{0:T(1024)S(1)}) all-reduce(f32[1024]{0:T(1024)S(1)} %get-tuple-element.76, f32[1024]{0:T(1024)S(1)} %get-tuple-element.75), channel_id=1, replica_groups=mesh['col'=4,'ta'=8] {'col','ta'}, use_global_device_ids=true, to_apply=%region_31.32 | all-reduce | flops 2048 | bytes 16384 | tf_op jit(solution)/shard_map/psum | solution.py:38
  907.7 12.4 multiply_convert_fusion.1
  920.1 8.9 fusion.73
  929.1 40.2 %all-reduce.16 = (f32[256]{0:T(256)S(1)}, f32[256]{0:T(256)S(1)}) all-reduce(f32[256]{0:T(256)S(1)} %get-tuple-element.154, f32[256]{0:T(256)S(1)} %get-tuple-element.153), channel_id=1, replica_groups=mesh['col'=4,'ta'=8] {'col','ta'}, use_global_device_ids=true, to_apply=%region_35.36 | all-reduce | flops 512 | bytes 4096 | tf_op jit(solution)/shard_map/psum | solution.py:38
  977.3 7.4 multiply_reduce_fusion.60
  989.9 22.5 %add_multiply_fusion.3 = f32[21,14,14,256]{3,2,1,0:T(8,128)} fusion(f32[21,14,14,256]{3,2,1,0:T(8,128)} %reshape.480, f32[256]{0:T(256)S(1)} %bitcast.336, f32[256]{0:T(256)S(1)} %bitcast.338, f32[256]{0:T(256)S(1)} %bitcast.340, f32[256]{0:T(256)S(1)} %bitcast.342, f32[256]{0:T(256)S(1)} %bitcast.344, f32[256]{0:T(256)S(1)} %bitcast.346, ...), kind=kLoop, calls=%fused_computation.151 | loop fusion | flops 18966528 | bytes 8438868 | tf_op jit(solution)/shard_map/mul | solution.py:271
  1019.7 20.2 %multiply_reduce_fusion.6 = (f32[256]{0:T(256)S(1)}, f32[256]{0:T(256)S(1)}, f32[256]{0:T(256)S(1)}, f32[256]{0:T(256)S(1)}, f32[256]{0:T(256)S(1)}, /*index=5*/...) fusion(f32[21,14,14,256]{3,2,1,0:T(8,128)S(1)} %copy-done.2, ...), kind=kLoop, calls=%fused_computation.98 | loop fusion | flops 37928704 | bytes 14769236 | tf_op jit(solution)/shard_map/reduce_sum | solution.py:88
  1039.9 8.5 fusion.21
  1069.9 12.7 convert_element_type.237
  1089.7 23.9 %fusion.2 = bf16[21,14,14,256]{3,2,1,0:T(8,128)(2,1)S(1)} fusion(f32[20,14,14,256]{3,2,1,0:T(8,128)} %slice.987, f32[1,14,14,256]{3,2,1,0:T(8,128)S(1)} %fusion.56, f32[21,14,14,256]{3,2,1,0:T(8,128)} %fusion.46, f32[21,14,14,256]{3,2,1,0:T(8,128)} %reshape.480, f32[256]{0:T(256)S(1)} %bitcast.316, f32[256]{0:T(256)S(1)} %bitcast.318, f32[256]{0:T(256)S(1)} %bitcast.320, ...), kind=kLoop, calls=%fused_computation.94 | loop fusion | flops 23181312 | bytes 14761044 | tf_op jit(solution)/shard_map/convert_element_type | solution.py:291
  1121.7 40.4 %all-reduce.15 = (f32[256]{0:T(256)S(1)}, f32[256]{0:T(256)S(1)}) all-reduce(f32[256]{0:T(256)S(1)} %get-tuple-element.152, f32[256]{0:T(256)S(1)} %get-tuple-element.151), channel_id=1, replica_groups=mesh['col'=4,'ta'=8] {'col','ta'}, use_global_device_ids=true, to_apply=%region_39.40 | all-reduce | flops 512 | bytes 4096 | tf_op jit(solution)/shard_map/psum | solution.py:38
  1167.2 22.6 %fusion.68 = (f32[1024]{0:T(1024)S(1)}, f32[1024]{0:T(1024)S(1)}, f32[4116,1024]{1,0:T(8,128)}) fusion(f32[1024]{0:T(1024)S(1)} %copy-done.48, f32[4116,1024]{1,0:T(8,128)} %get-tuple-element.279, f32[1024]{0:T(1024)S(1)} %copy-done.44, f32[1024]{0:T(1024)S(1)} %bitcast.255, f32[1024]{0:T(1024)S(1)} %bitcast.251, bf16[4116,1024]{1,0:T(8,128)(2,1)} %reshape.475, ...), kind=kOutput, calls=%fused_computation.335 | convolution fusion | flops 2233833472 | bytes 61665280 | tf_op jit(solution)/shard_map/vb,db->vd/dot_general | solution.py:312
  1189.8 40.0 %all-reduce.14 = (f32[1024]{0:T(1024)S(1)}, f32[1024]{0:T(1024)S(1)}) all-reduce(f32[1024]{0:T(1024)S(1)} %get-tuple-element.74, f32[1024]{0:T(1024)S(1)} %get-tuple-element.73), channel_id=1, replica_groups=mesh['col'=4,'ta'=8] {'col','ta'}, use_global_device_ids=true, to_apply=%region_43.44 | all-reduce | flops 2048 | bytes 16384 | tf_op jit(solution)/shard_map/psum | solution.py:38
  1229.9 12.6 multiply_convert_fusion
  1242.5 8.9 fusion.71
  1251.4 40.2 %all-reduce.13 = (f32[256]{0:T(256)S(1)}, f32[256]{0:T(256)S(1)}) all-reduce(f32[256]{0:T(256)S(1)} %get-tuple-element.150, f32[256]{0:T(256)S(1)} %get-tuple-element.149), channel_id=1, replica_groups=mesh['col'=4,'ta'=8] {'col','ta'}, use_global_device_ids=true, to_apply=%region_47.48 | all-reduce | flops 512 | bytes 4096 | tf_op jit(solution)/shard_map/psum | solution.py:38
  1304.8 30.4 %multiply_reduce_fusion.31 = (f32[256]{0:T(256)S(1)}, f32[256]{0:T(256)S(1)}, f32[256]{0:T(256)S(1)}, f32[256]{0:T(256)S(1)}, f32[256]{0:T(256)S(1)}, /*index=5*...) fusion(f32[21,14,14,256]{3,2,1,0:T(8,128)} %reshape.482, ...), kind=kLoop, calls=%fused_computation.123 | loop fusion | flops 37928704 | bytes 14769236 | tf_op jit(solution)/shard_map/reduce_sum | solution.py:88
  1362.5 8.5 fusion.22
  1394.3 24.1 %fusion.4 = bf16[21,14,14,256]{3,2,1,0:T(8,128)(2,1)} fusion(f32[20,14,14,256]{3,2,1,0:T(8,128)} %slice.990, f32[1,14,14,256]{3,2,1,0:T(8,128)} %fusion.55, f32[21,14,14,256]{3,2,1,0:T(8,128)S(1)} %fusion.45, f32[21,14,14,256]{3,2,1,0:T(8,128)} %reshape.482, f32[21]{0:T(128)S(1)} %fusion.67, f32[256]{0:T(256)S(1)} %bitcast.262, f32[256]{0:T(256)} %bitcast.264, ...), kind=kLoop, calls=%fused_computation.97 | loop fusion | flops 23181312 | bytes 14761044 | tf_op jit(solution)/shard_map/convert_element_type | solution.py:291
  1428.1 40.8 %all-reduce.12 = (f32[256]{0:T(256)S(1)}, f32[256]{0:T(256)S(1)}, f32[2,27,256]{2,1,0:T(8,128)S(1)}) all-reduce(f32[256]{0:T(256)S(1)} %get-tuple-element.148, f32[256]{0:T(256)S(1)} %get-tuple-element.147, f32[2,27,256]{2,1,0:T(8,128)S(1)} %copy-done.39), channel_id=1, replica_groups=mesh['col'=4,'ta'=8] {'col','ta'}, use_global_device_ids=true, to_apply=%region_51.52 | all-reduce | flops 14336 | bytes 114688 | tf_op jit(solution)/shard_map/psum | solution.py:38
  1481.8 11.4 add_convert_fusion
  1493.2 12.8 convert_element_type.251
  1507.9 14.3 broadcast_select_fusion
  1522.2 105.4 %all-reduce.21.cloned.1.call-done = (f32[2,1024,256]{1,2,0:T(8,128)}, f32[2,256,256]{2,1,0:T(8,128)}, f32[2,256,1024]{2,1,0:T(8,128)}) async-done(((f32[2,1024,256]{1,2,0:T(8,128)}, f32[2,256,256]{2,1,0:T(8,128)}, f32[2,256,1024]{2,1,0:T(8,128)}), (f32[2,1024,256]{1,2,0:T(8,128)}, f32[2,256,256]{2,1,0:T(8,128)}, f32[2,256,1024]{2,1,0:T(8,128)})) %all-reduce.21.cloned.1.call-update) | async-done | bytes 4718608 | tf_op jit(solution)/shard_map/psum | solution.py:329
  (458 shorter events, 284.1 us)
Async XLA Ops:
  7.2 1620.4 %all-reduce.21.cloned.1.call-start = ((), (), s32[]{:S(2)}) async-start(), calls=%async_computation | async-start | bytes 9437184 | tf_op jit(solution)/shard_map/psum | solution.py:329
  22.9 93.4 %copy-start.133 = (bf16[2,2,256]{2,1,0:T(2,128)(2,1)S(1)}, bf16[2,2,256]{2,1,0:T(2,128)(2,1)}, u32[]{:S(2)}) copy-start(bf16[2,2,256]{2,1,0:T(2,128)(2,1)} %param.20) | copy-start | bytes 6148
  22.9 93.4 %copy-start.134 = (bf16[2,2,256]{2,1,0:T(2,128)(2,1)S(1)}, bf16[2,2,256]{2,1,0:T(2,128)(2,1)}, u32[]{:S(2)}) copy-start(bf16[2,2,256]{2,1,0:T(2,128)(2,1)} %param.21) | copy-start | bytes 6148
  72.7 48.9 %copy-start.49 = (f32[256]{0:T(256)}, f32[256]{0:T(256)S(1)}, u32[]{:S(2)}) copy-start(f32[256]{0:T(256)S(1)} %broadcast_multiply_fusion.13) | copy-start | bytes 3076
  72.7 50.2 %copy-start.36 = (bf16[2,256,256]{2,1,0:T(8,128)(2,1)S(1)}, bf16[2,256,256]{2,1,0:T(8,128)(2,1)}, u32[]{:S(2)}) copy-start(bf16[2,256,256]{2,1,0:T(8,128)(2,1)} %param.17) | copy-start | bytes 786436
  116.9 215.8 %copy-start.118 = (f32[1,1,256]{2,1,0:T(1,128)}, f32[1,1,256]{2,1,0:T(1,128)S(1)}, u32[]{:S(2)}) copy-start(f32[1,1,256]{2,1,0:T(1,128)S(1)} %get-tuple-element.302) | copy-start | bytes 3076
  126.7 55.2 %collective-permute-start = (bf16[1,14,14,256]{3,2,1,0:T(8,128)(2,1)S(1)}, bf16[1,14,14,256]{3,2,1,0:T(8,128)(2,1)S(1)}, u32[]{:S(2)}, u32[]{:S(2)}) collective-permute-start(bf16[1,14,14,256]{3,2,1,0:T(8,128)(2,1)S(1)} %constant_dynamic-slice_fusion.4), channel_id=1, source_target_pairs={{0,1},{1,2},{2,3},{3,4},{4,5},{5,6},{6,7},{8,9},{9,10},{10,11},{11... | collective-permute-start | bytes 301064 | tf_op jit(solution)/shard_map/ppermute | solution.py:17
  128.1 50.8 %collective-permute-start.1 = (bf16[1,14,14,256]{3,2,1,0:T(8,128)(2,1)S(1)}, bf16[1,14,14,256]{3,2,1,0:T(8,128)(2,1)S(1)}, u32[]{:S(2)}, u32[]{:S(2)}) collective-permute-start(bf16[1,14,14,256]{3,2,1,0:T(8,128)(2,1)S(1)} %slice.781), channel_id=1, source_target_pairs={{1,0},{2,1},{3,2},{4,3},{5,4},{6,5},{7,6},{9,8},{10,9},{11,10},{12... | collective-permute-start | bytes 301064 | tf_op jit(solution)/shard_map/ppermute | solution.py:18
  133.5 51.5 %copy-start.64 = (f32[1,1,256]{2,0,1:T(1,128)}, f32[1,1,256]{2,0,1:T(1,128)S(1)}, u32[]{:S(2)}) copy-start(f32[1,1,256]{2,0,1:T(1,128)S(1)} %get-tuple-element.229) | copy-start | bytes 3076
  133.5 51.5 %copy-start.66 = (f32[1,1,256]{2,0,1:T(1,128)}, f32[1,1,256]{2,0,1:T(1,128)S(1)}, u32[]{:S(2)}) copy-start(f32[1,1,256]{2,0,1:T(1,128)S(1)} %get-tuple-element.230) | copy-start | bytes 3076
  133.5 51.5 %copy-start.67 = (f32[1,1,256]{2,0,1:T(1,128)}, f32[1,1,256]{2,0,1:T(1,128)S(1)}, u32[]{:S(2)}) copy-start(f32[1,1,256]{2,0,1:T(1,128)S(1)} %get-tuple-element.231) | copy-start | bytes 3076
  133.5 51.5 %copy-start.68 = (f32[1,1,256]{2,0,1:T(1,128)}, f32[1,1,256]{2,0,1:T(1,128)S(1)}, u32[]{:S(2)}) copy-start(f32[1,1,256]{2,0,1:T(1,128)S(1)} %get-tuple-element.232) | copy-start | bytes 3076
  133.5 51.5 %copy-start.69 = (f32[1,1,256]{2,0,1:T(1,128)}, f32[1,1,256]{2,0,1:T(1,128)S(1)}, u32[]{:S(2)}) copy-start(f32[1,1,256]{2,0,1:T(1,128)S(1)} %get-tuple-element.233) | copy-start | bytes 3076
  133.5 51.5 %copy-start.70 = (f32[1,1,256]{2,0,1:T(1,128)}, f32[1,1,256]{2,0,1:T(1,128)S(1)}, u32[]{:S(2)}) copy-start(f32[1,1,256]{2,0,1:T(1,128)S(1)} %get-tuple-element.234) | copy-start | bytes 3076
  133.5 51.5 %copy-start.71 = (f32[1,1,256]{2,0,1:T(1,128)}, f32[1,1,256]{2,0,1:T(1,128)S(1)}, u32[]{:S(2)}) copy-start(f32[1,1,256]{2,0,1:T(1,128)S(1)} %get-tuple-element.235) | copy-start | bytes 3076
  133.5 51.5 %copy-start.72 = (f32[1,1,256]{2,0,1:T(1,128)}, f32[1,1,256]{2,0,1:T(1,128)S(1)}, u32[]{:S(2)}) copy-start(f32[1,1,256]{2,0,1:T(1,128)S(1)} %get-tuple-element.236) | copy-start | bytes 3076
  133.5 51.5 %copy-start.73 = (f32[1,1,256]{2,0,1:T(1,128)}, f32[1,1,256]{2,0,1:T(1,128)S(1)}, u32[]{:S(2)}) copy-start(f32[1,1,256]{2,0,1:T(1,128)S(1)} %get-tuple-element.237) | copy-start | bytes 3076
  133.6 51.5 %copy-start.74 = (f32[1,1,256]{2,0,1:T(1,128)}, f32[1,1,256]{2,0,1:T(1,128)S(1)}, u32[]{:S(2)}) copy-start(f32[1,1,256]{2,0,1:T(1,128)S(1)} %get-tuple-element.220) | copy-start | bytes 3076
  133.6 51.5 %copy-start.76 = (f32[1,1,256]{2,0,1:T(1,128)}, f32[1,1,256]{2,0,1:T(1,128)S(1)}, u32[]{:S(2)}) copy-start(f32[1,1,256]{2,0,1:T(1,128)S(1)} %get-tuple-element.221) | copy-start | bytes 3076
  133.6 51.5 %copy-start.78 = (f32[1,1,256]{2,0,1:T(1,128)}, f32[1,1,256]{2,0,1:T(1,128)S(1)}, u32[]{:S(2)}) copy-start(f32[1,1,256]{2,0,1:T(1,128)S(1)} %get-tuple-element.222) | copy-start | bytes 3076
  133.6 51.5 %copy-start.80 = (f32[1,1,256]{2,0,1:T(1,128)}, f32[1,1,256]{2,0,1:T(1,128)S(1)}, u32[]{:S(2)}) copy-start(f32[1,1,256]{2,0,1:T(1,128)S(1)} %get-tuple-element.223) | copy-start | bytes 3076
  133.6 51.5 %copy-start.82 = (f32[1,1,256]{2,0,1:T(1,128)}, f32[1,1,256]{2,0,1:T(1,128)S(1)}, u32[]{:S(2)}) copy-start(f32[1,1,256]{2,0,1:T(1,128)S(1)} %get-tuple-element.224) | copy-start | bytes 3076
  133.6 51.5 %copy-start.84 = (f32[1,1,256]{2,0,1:T(1,128)}, f32[1,1,256]{2,0,1:T(1,128)S(1)}, u32[]{:S(2)}) copy-start(f32[1,1,256]{2,0,1:T(1,128)S(1)} %get-tuple-element.225) | copy-start | bytes 3076
  133.6 51.5 %copy-start.86 = (f32[1,1,256]{2,0,1:T(1,128)}, f32[1,1,256]{2,0,1:T(1,128)S(1)}, u32[]{:S(2)}) copy-start(f32[1,1,256]{2,0,1:T(1,128)S(1)} %get-tuple-element.226) | copy-start | bytes 3076
  133.6 51.5 %copy-start.88 = (f32[1,1,256]{2,0,1:T(1,128)}, f32[1,1,256]{2,0,1:T(1,128)S(1)}, u32[]{:S(2)}) copy-start(f32[1,1,256]{2,0,1:T(1,128)S(1)} %get-tuple-element.227) | copy-start | bytes 3076
  133.6 51.5 %copy-start.90 = (f32[1,1,256]{2,0,1:T(1,128)}, f32[1,1,256]{2,0,1:T(1,128)S(1)}, u32[]{:S(2)}) copy-start(f32[1,1,256]{2,0,1:T(1,128)S(1)} %get-tuple-element.228) | copy-start | bytes 3076
  133.6 51.5 %copy-start.92 = (f32[1,1,256]{2,0,1:T(1,128)}, f32[1,1,256]{2,0,1:T(1,128)S(1)}, u32[]{:S(2)}) copy-start(f32[1,1,256]{2,0,1:T(1,128)S(1)} %get-tuple-element.219) | copy-start | bytes 3076
  133.7 51.5 %copy-start.94 = (f32[1,1,256]{2,0,1:T(1,128)}, f32[1,1,256]{2,0,1:T(1,128)S(1)}, u32[]{:S(2)}) copy-start(f32[1,1,256]{2,0,1:T(1,128)S(1)} %get-tuple-element.291) | copy-start | bytes 3076
  133.7 51.5 %copy-start.96 = (f32[1,1,256]{2,0,1:T(1,128)}, f32[1,1,256]{2,0,1:T(1,128)S(1)}, u32[]{:S(2)}) copy-start(f32[1,1,256]{2,0,1:T(1,128)S(1)} %get-tuple-element.292) | copy-start | bytes 3076
  133.7 51.5 %copy-start.98 = (f32[1,1,256]{2,0,1:T(1,128)}, f32[1,1,256]{2,0,1:T(1,128)S(1)}, u32[]{:S(2)}) copy-start(f32[1,1,256]{2,0,1:T(1,128)S(1)} %get-tuple-element.293) | copy-start | bytes 3076
  133.7 51.5 %copy-start.100 = (f32[1,1,256]{2,0,1:T(1,128)}, f32[1,1,256]{2,0,1:T(1,128)S(1)}, u32[]{:S(2)}) copy-start(f32[1,1,256]{2,0,1:T(1,128)S(1)} %get-tuple-element.294) | copy-start | bytes 3076
  133.7 51.5 %copy-start.102 = (f32[1,1,256]{2,0,1:T(1,128)}, f32[1,1,256]{2,0,1:T(1,128)S(1)}, u32[]{:S(2)}) copy-start(f32[1,1,256]{2,0,1:T(1,128)S(1)} %get-tuple-element.295) | copy-start | bytes 3076
  133.7 51.5 %copy-start.104 = (f32[1,1,256]{2,0,1:T(1,128)}, f32[1,1,256]{2,0,1:T(1,128)S(1)}, u32[]{:S(2)}) copy-start(f32[1,1,256]{2,0,1:T(1,128)S(1)} %get-tuple-element.296) | copy-start | bytes 3076
  133.7 51.5 %copy-start.106 = (f32[1,1,256]{2,0,1:T(1,128)}, f32[1,1,256]{2,0,1:T(1,128)S(1)}, u32[]{:S(2)}) copy-start(f32[1,1,256]{2,0,1:T(1,128)S(1)} %get-tuple-element.297) | copy-start | bytes 3076
  133.7 51.5 %copy-start.108 = (f32[1,1,256]{2,0,1:T(1,128)}, f32[1,1,256]{2,0,1:T(1,128)S(1)}, u32[]{:S(2)}) copy-start(f32[1,1,256]{2,0,1:T(1,128)S(1)} %get-tuple-element.298) | copy-start | bytes 3076
  134.9 301.4 %copy-start.45 = (f32[1,1024]{1,0:T(1,128)}, f32[1,1024]{1,0:T(1,128)S(1)}, u32[]{:S(2)}) copy-start(f32[1,1024]{1,0:T(1,128)S(1)} %get-tuple-element.251) | copy-start | bytes 12292
  134.9 301.3 %copy-start.55 = (f32[1,1024]{1,0:T(1,128)}, f32[1,1024]{1,0:T(1,128)S(1)}, u32[]{:S(2)}) copy-start(f32[1,1024]{1,0:T(1,128)S(1)} %get-tuple-element.253) | copy-start | bytes 12292
  288.3 48.2 %copy-start.51 = (f32[256]{0:T(256)}, f32[256]{0:T(256)S(1)}, u32[]{:S(2)}) copy-start(f32[256]{0:T(256)S(1)} %broadcast_multiply_fusion.12) | copy-start | bytes 3076
  564.3 19.6 %collective-permute-start.2 = (bf16[1,14,14,256]{3,2,1,0:T(8,128)(2,1)S(1)}, bf16[1,14,14,256]{3,2,1,0:T(8,128)(2,1)S(1)}, u32[]{:S(2)}, u32[]{:S(2)}) collective-permute-start(bf16[1,14,14,256]{3,2,1,0:T(8,128)(2,1)S(1)} %constant_dynamic-slice_fusion.3), channel_id=1, source_target_pairs={{0,1},{1,2},{2,3},{3,4},{4,5},{5,6},{6,7},{8,9},{9,10},{10,11},{11... | collective-permute-start | bytes 301064 | tf_op jit(solution)/shard_map/ppermute | solution.py:17
  565.6 15.3 collective-permute-start.3
  920.1 49.1 %copy-start.12 = (bf16[20,14,14,256]{3,2,1,0:T(8,128)(2,1)S(1)}, bf16[20,14,14,256]{3,2,1,0:T(8,128)(2,1)}, u32[]{:S(2)}) copy-start(bf16[20,14,14,256]{3,2,1,0:T(8,128)(2,1)} %slice.812) | copy-start | bytes 6021124
  1049.4 38.6 %collective-permute-start.5 = (bf16[1,14,14,256]{3,2,1,0:T(8,128)(2,1)S(1)}, bf16[1,14,14,256]{3,2,1,0:T(8,128)(2,1)S(1)}, u32[]{:S(2)}, u32[]{:S(2)}) collective-permute-start(bf16[1,14,14,256]{3,2,1,0:T(8,128)(2,1)S(1)} %slice.1406), channel_id=1, source_target_pairs={{1,0},{2,1},{3,2},{4,3},{5,4},{6,5},{7,6},{9,8},{10,9},{11,10},{12... | collective-permute-start | bytes 301064 | tf_op jit(solution)/shard_map/ppermute | solution.py:18
  1051.6 36.3 %collective-permute-start.4 = (bf16[1,14,14,256]{3,2,1,0:T(8,128)(2,1)S(1)}, bf16[1,14,14,256]{3,2,1,0:T(8,128)(2,1)S(1)}, u32[]{:S(2)}, u32[]{:S(2)}) collective-permute-start(bf16[1,14,14,256]{3,2,1,0:T(8,128)(2,1)S(1)} %dynamic-slice_convert_fusion.1), channel_id=1, source_target_pairs={{0,1},{1,2},{2,3},{3,4},{4,5},{5,6},{6,7},{8,9},{9,10},{10,11},{11... | collective-permute-start | bytes 301064 | tf_op jit(solution)/shard_map/ppermute | solution.py:17
  1167.2 62.7 %copy-start.61 = (f32[1024]{0:T(1024)S(1)}, f32[1024]{0:T(1024)}, u32[]{:S(2)}) copy-start(f32[1024]{0:T(1024)} %get-tuple-element.246) | copy-start | bytes 12292
  1242.5 49.6 %copy-start.4 = (bf16[4116,256]{1,0:T(8,128)(2,1)S(1)}, bf16[4116,256]{1,0:T(8,128)(2,1)}, u32[]{:S(2)}) copy-start(bf16[4116,256]{1,0:T(8,128)(2,1)} %copy-done.3) | copy-start | bytes 6322180
  1242.5 49.6 %copy-start.121 = (f32[256]{0:T(256)S(1)}, f32[256]{0:T(256)}, u32[]{:S(2)}) copy-start(f32[256]{0:T(256)} %get-tuple-element.268) | copy-start | bytes 3076
  1379.7 11.9 collective-permute-start.7
  1381.1 10.5 collective-permute-start.6
  (111 other events, 1283.3 us)
Sparse Core Ops, SparseCore 0:
  1481.9 145.6 all-reduce.20
where the time goes:
time: 1650 us; the launch traced here: 1640 us
  blocking collectives  731 us (44%)
  other arithmetic  475 us (29%)
  local copies, waits for them, and re-layouts  171 us (10%)
  matrix products  126 us (8%)
  waiting for transfers between devices  105 us (6%)
  between operations  17.1 us (1%)
    psum x6, blocking collectives, normalize(): lax.psum(jnp.sum(values * alive_rows, axis=0), ('col', 'ta')) / summed_count  249 us
    psum x6, blocking collectives, normalize_back(): lax.psum((jnp.sum(grad_z, axis=0), jnp.sum(grad_z * normed, axis=0)), ('c...  242 us
    psum x6, blocking collectives, normalize(): lax.psum(jnp.sum(centred * centred * alive_rows, axis=0), ('col', 'ta'))  241 us
    reduce_sum x2, other arithmetic, normalize(): jnp.sum(values * alive_rows, axis=0)  119 us
    psum x1, waiting for transfers between devices, body(): lax.psum((jnp.stack(grads_reduce[::-1]), jnp.stack(grads_mid[::-1]), jnp....  105 us
    reduce_sum x6, other arithmetic, spatial_kernel_grad(): jnp.sum(grid_grad * padded[:, row_off:row_off + span_h, col_off:col_off +...  78.9 us
    convert_element_type x2, other arithmetic, body(): grad_h2 = ((toward_self + from_later + from_earlier) * alive_grid).reshap...  48 us
    dot_general x2, matrix products, body(): jnp.einsum('vb,db->vd', grad_h1_low, w_reduce[block_id], preferred_elemen...  34.1 us
  transfers between devices with their start and end apart: 9, of which 1 were waited for; matrix products, arithmetic and copies ran while one was open for 9% of the time, Pallas kernels for 0%

commit v1 on v0

--- a/solution.py
+++ b/solution.py
@@ -26,7 +26,7 @@
 
 
 def normalize(values, alive_rows, summed_count, gain_vec, bias_vec):
-    average = lax.psum(jnp.sum(values * alive_rows, axis=0), ("col", "ta")) / summed_count
+    average = lax.psum(lax.psum(jnp.sum(values * alive_rows, axis=0), "ta"), "col") / summed_count
     centred = values - average
     spread = lax.psum(jnp.sum(centred * centred * alive_rows, axis=0), ("col", "ta")) / summed_count
     inverse = lax.rsqrt(spread + EPS)

time: 1650 us -> 1540 us (0.933)
  blocking collectives: 731 us -> 621 us
    psum x6 -> x12, blocking collectives: 249 us -> 156 us  [the longest x6 96.3 us: normalize(): lax.psum(jnp.sum(values * alive_rows, axis=0), 'ta')]
    psum x6, blocking collectives: 241 us -> 223 us  [normalize(): lax.psum(jnp.sum(centred * centred * alive_rows, axis=0), ('col', 'ta'))]
  transfers between devices with their start and end apart: 9 -> 9, of which waited for: 1 -> 1; matrix products, arithmetic and copies ran while one was open for 9% -> 10% of each run, Pallas kernels for 0% -> 0%
where the time goes in v1:
time: 1540 us; the launch traced here: 1530 us
  blocking collectives  621 us (40%)
  other arithmetic  475 us (31%)
  local copies, waits for them, and re-layouts  170 us (11%)
  matrix products  126 us (8%)
  waiting for transfers between devices  105 us (7%)
  between operations  17.1 us (1%)
    psum x6, blocking collectives, normalize_back(): lax.psum((jnp.sum(grad_z, axis=0), jnp.sum(grad_z * normed, axis=0)), ('c...  242 us
    psum x6, blocking collectives, normalize(): lax.psum(jnp.sum(centred * centred * alive_rows, axis=0), ('col', 'ta'))  223 us
    reduce_sum x2, other arithmetic, normalize(): jnp.sum(values * alive_rows, axis=0)  119 us
    psum x1, waiting for transfers between devices, body(): lax.psum((jnp.stack(grads_reduce[::-1]), jnp.stack(grads_mid[::-1]), jnp....  105 us
    psum x6, blocking collectives, normalize(): lax.psum(jnp.sum(values * alive_rows, axis=0), 'ta')  96.3 us
    reduce_sum x6, other arithmetic, spatial_kernel_grad(): jnp.sum(grid_grad * padded[:, row_off:row_off + span_h, col_off:col_off +...  78.9 us
    psum x6, blocking collectives, normalize(): lax.psum(lax.psum(jnp.sum(values * alive_rows, axis=0), 'ta'), 'col')  59.4 us
    convert_element_type x2, other arithmetic, body(): grad_h2 = ((toward_self + from_later + from_earlier) * alive_grid).reshap...  48 us
  transfers between devices with their start and end apart: 9, of which 1 were waited for; matrix products, arithmetic and copies ran while one was open for 10% of the time, Pallas kernels for 0%

profile of v1, /device:TPU:0, one launch (start us, length us, event | category | flops | bytes accessed | tf_op | source)
XLA Modules:
  0.0 1530.7 jit_solution(5443210475737293404)
XLA Ops:
  10.0 12.9 reshape.475
  30.7 18.1 %psum.238 = f32[256]{0:T(256)S(1)} all-reduce(f32[256]{0:T(256)S(1)} %get-tuple-element.276), channel_id=1, replica_groups=mesh['col'=4,'ta'=8] {'ta'}, use_global_device_ids=true, to_apply=%region_1.2 | all-reduce | flops 256 | bytes 2048 | tf_op jit(solution)/shard_map/psum | solution.py:29
  48.8 9.9 psum.239
  62.1 36.9 %psum.240 = f32[256]{0:T(256)S(1)} all-reduce(f32[256]{0:T(256)S(1)} %multiply_reduce_fusion.70), channel_id=1, replica_groups=mesh['col'=4,'ta'=8] {'col','ta'}, use_global_device_ids=true, to_apply=%region_4.5 | all-reduce | flops 256 | bytes 2048 | tf_op jit(solution)/shard_map/psum | solution.py:31
  117.7 11.8 select_convert_fusion
  140.3 18.5 %reshape.564 = f32[4116,1024]{1,0:T(8,128)} reshape(f32[21,14,14,1024]{3,2,1,0:T(8,128)} %select_convert_fusion) | data formatting | bytes 33718272 | tf_op jit(solution)/shard_map/convert_element_type | solution.py:216
  168.0 60.1 %multiply_reduce_fusion.59 = (f32[256]{0:T(256)S(1)}, f32[21,14,14,256]{3,2,1,0:T(8,128)}) fusion(f32[21]{0:T(128)S(1)} %fusion.67, f32[256]{0:T(256)S(1)} %bitcast.279, f32[256]{0:T(256)S(1)} %bitcast.281, f32[256]{0:T(256)S(1)} %bitcast.283, f32[256]{0:T(256)S(1)} %bitcast.285, f32[21,14,14,256]{3,2,1,0:T(8,128)} %convert_multiply_fusion.1, ...), kind=kLoop, calls=%fused_computation.159 | loop fusion | flops 57953024 | bytes 16887892 | tf_op jit(solution)/shard_map/reduce_sum | solution.py:29
  228.1 17.8 %psum.241 = f32[256]{0:T(256)S(1)} all-reduce(f32[256]{0:T(256)S(1)} %get-tuple-element.178), channel_id=1, replica_groups=mesh['col'=4,'ta'=8] {'ta'}, use_global_device_ids=true, to_apply=%region_10.11 | all-reduce | flops 256 | bytes 2048 | tf_op jit(solution)/shard_map/psum | solution.py:29
  245.9 9.7 psum.242
  259.0 37.3 %psum.243 = f32[256]{0:T(256)S(1)} all-reduce(f32[256]{0:T(256)S(1)} %multiply_reduce_fusion.58), channel_id=1, replica_groups=mesh['col'=4,'ta'=8] {'col','ta'}, use_global_device_ids=true, to_apply=%region_13.14 | all-reduce | flops 256 | bytes 2048 | tf_op jit(solution)/shard_map/psum | solution.py:31
  302.7 9.8 multiply_reduce_fusion.5
  312.5 14.5 psum.244
  326.9 9.7 psum.245
  344.0 37.3 %psum.246 = f32[1024]{0:T(1024)S(1)} all-reduce(f32[1024]{0:T(1024)S(1)} %multiply_reduce_fusion.4), channel_id=1, replica_groups=mesh['col'=4,'ta'=8] {'col','ta'}, use_global_device_ids=true, to_apply=%region_18.19 | all-reduce | flops 1024 | bytes 8192 | tf_op jit(solution)/shard_map/psum | solution.py:31
  382.0 10.9 fusion
  399.9 14.1 psum.247
  414.0 9.7 psum.248
  427.1 37.5 %psum.249 = f32[256]{0:T(256)S(1)} all-reduce(f32[256]{0:T(256)S(1)} %multiply_reduce_fusion.68), channel_id=1, replica_groups=mesh['col'=4,'ta'=8] {'col','ta'}, use_global_device_ids=true, to_apply=%region_23.24 | all-reduce | flops 256 | bytes 2048 | tf_op jit(solution)/shard_map/psum | solution.py:31
  514.0 59.2 %multiply_reduce_fusion.57 = (f32[256]{0:T(256)S(1)}, f32[21,14,14,256]{3,2,1,0:T(8,128)}) fusion(f32[21]{0:T(128)S(1)} %fusion.67, f32[256]{0:T(256)S(1)} %bitcast.349, f32[256]{0:T(256)S(1)} %bitcast.351, f32[256]{0:T(256)S(1)} %bitcast.353, f32[256]{0:T(256)S(1)} %bitcast.355, f32[21,14,14,256]{3,2,1,0:T(8,128)} %convert_multiply_fusion, ...), kind=kLoop, calls=%fused_computation.154 | loop fusion | flops 57953024 | bytes 16887892 | tf_op jit(solution)/shard_map/reduce_sum | solution.py:29
  573.2 17.4 %psum.250 = f32[256]{0:T(256)S(1)} all-reduce(f32[256]{0:T(256)S(1)} %get-tuple-element.176), channel_id=1, replica_groups=mesh['col'=4,'ta'=8] {'ta'}, use_global_device_ids=true, to_apply=%region_25.26 | all-reduce | flops 256 | bytes 2048 | tf_op jit(solution)/shard_map/psum | solution.py:29
  590.5 10.6 psum.251
  609.8 37.3 %psum.252 = f32[256]{0:T(256)S(1)} all-reduce(f32[256]{0:T(256)S(1)} %multiply_reduce_fusion.56), channel_id=1, replica_groups=mesh['col'=4,'ta'=8] {'col','ta'}, use_global_device_ids=true, to_apply=%region_28.29 | all-reduce | flops 256 | bytes 2048 | tf_op jit(solution)/shard_map/psum | solution.py:31
  652.9 9.8 multiply_reduce_fusion.3
  662.7 14.5 psum.253
  677.1 9.7 psum.254
  694.2 36.9 %psum.255 = f32[1024]{0:T(1024)S(1)} all-reduce(f32[1024]{0:T(1024)S(1)} %multiply_reduce_fusion.2), channel_id=1, replica_groups=mesh['col'=4,'ta'=8] {'col','ta'}, use_global_device_ids=true, to_apply=%region_33.34 | all-reduce | flops 1024 | bytes 8192 | tf_op jit(solution)/shard_map/psum | solution.py:31
  731.1 25.8 %fusion.69 = (f32[1024]{0:T(1024)S(1)}, f32[1024]{0:T(1024)S(1)}, f32[4116,1024]{1,0:T(8,128)}, bf16[4116,1024]{1,0:T(8,128)(2,1)}) fusion(f32[1024]{0:T(1024)S(1)} %get-tuple-element.249, f32[4116,1024]{1,0:T(8,128)} %get-tuple-element.283, f32[1024]{0:T(1024)S(1)} %broadcast_multiply_fusion.4, f32[4116,1024]{1,0:T(8,128)} %reshape.564, ...), kind=kLoop, calls=%fused_computation.336 | loop fusion | flops 75864064 | bytes 75890688 | tf_op jit(solution)/shard_map/reduce_sum | solution.py:39
  756.9 41.5 %all-reduce.17 = (f32[1024]{0:T(1024)S(1)}, f32[1024]{0:T(1024)S(1)}) all-reduce(f32[1024]{0:T(1024)S(1)} %get-tuple-element.76, f32[1024]{0:T(1024)S(1)} %get-tuple-element.75), channel_id=1, replica_groups=mesh['col'=4,'ta'=8] {'col','ta'}, use_global_device_ids=true, to_apply=%region_37.38 | all-reduce | flops 2048 | bytes 16384 | tf_op jit(solution)/shard_map/psum | solution.py:38
  798.4 12.4 multiply_convert_fusion.1
  810.8 8.9 fusion.73
  819.7 39.5 %all-reduce.16 = (f32[256]{0:T(256)S(1)}, f32[256]{0:T(256)S(1)}) all-reduce(f32[256]{0:T(256)S(1)} %get-tuple-element.154, f32[256]{0:T(256)S(1)} %get-tuple-element.153), channel_id=1, replica_groups=mesh['col'=4,'ta'=8] {'col','ta'}, use_global_device_ids=true, to_apply=%region_41.42 | all-reduce | flops 512 | bytes 4096 | tf_op jit(solution)/shard_map/psum | solution.py:38
  879.9 22.5 %add_multiply_fusion.3 = f32[21,14,14,256]{3,2,1,0:T(8,128)} fusion(f32[21,14,14,256]{3,2,1,0:T(8,128)} %reshape.480, f32[256]{0:T(256)S(1)} %bitcast.336, f32[256]{0:T(256)S(1)} %bitcast.338, f32[256]{0:T(256)S(1)} %bitcast.340, f32[256]{0:T(256)S(1)} %bitcast.342, f32[256]{0:T(256)S(1)} %bitcast.344, f32[256]{0:T(256)S(1)} %bitcast.346, ...), kind=kLoop, calls=%fused_computation.151 | loop fusion | flops 18966528 | bytes 8438868 | tf_op jit(solution)/shard_map/mul | solution.py:271
  909.7 20.2 %multiply_reduce_fusion.6 = (f32[256]{0:T(256)S(1)}, f32[256]{0:T(256)S(1)}, f32[256]{0:T(256)S(1)}, f32[256]{0:T(256)S(1)}, f32[256]{0:T(256)S(1)}, /*index=5*/...) fusion(f32[21,14,14,256]{3,2,1,0:T(8,128)S(1)} %copy-done.2, ...), kind=kLoop, calls=%fused_computation.98 | loop fusion | flops 37928704 | bytes 14769236 | tf_op jit(solution)/shard_map/reduce_sum | solution.py:88
  959.9 12.7 convert_element_type.237
  979.7 23.9 %fusion.2 = bf16[21,14,14,256]{3,2,1,0:T(8,128)(2,1)S(1)} fusion(f32[20,14,14,256]{3,2,1,0:T(8,128)} %slice.987, f32[1,14,14,256]{3,2,1,0:T(8,128)S(1)} %fusion.56, f32[21,14,14,256]{3,2,1,0:T(8,128)} %fusion.46, f32[21,14,14,256]{3,2,1,0:T(8,128)} %reshape.480, f32[256]{0:T(256)S(1)} %bitcast.316, f32[256]{0:T(256)S(1)} %bitcast.318, f32[256]{0:T(256)S(1)} %bitcast.320, ...), kind=kLoop, calls=%fused_computation.94 | loop fusion | flops 23181312 | bytes 14761044 | tf_op jit(solution)/shard_map/convert_element_type | solution.py:291
  1011.7 41.0 %all-reduce.15 = (f32[256]{0:T(256)S(1)}, f32[256]{0:T(256)S(1)}) all-reduce(f32[256]{0:T(256)S(1)} %get-tuple-element.152, f32[256]{0:T(256)S(1)} %get-tuple-element.151), channel_id=1, replica_groups=mesh['col'=4,'ta'=8] {'col','ta'}, use_global_device_ids=true, to_apply=%region_45.46 | all-reduce | flops 512 | bytes 4096 | tf_op jit(solution)/shard_map/psum | solution.py:38
  1057.8 22.6 %fusion.68 = (f32[1024]{0:T(1024)S(1)}, f32[1024]{0:T(1024)S(1)}, f32[4116,1024]{1,0:T(8,128)}) fusion(f32[1024]{0:T(1024)S(1)} %copy-done.48, f32[4116,1024]{1,0:T(8,128)} %get-tuple-element.279, f32[1024]{0:T(1024)S(1)} %copy-done.44, f32[1024]{0:T(1024)S(1)} %bitcast.255, f32[1024]{0:T(1024)S(1)} %bitcast.251, bf16[4116,1024]{1,0:T(8,128)(2,1)} %reshape.475, ...), kind=kOutput, calls=%fused_computation.335 | convolution fusion | flops 2233833472 | bytes 61665280 | tf_op jit(solution)/shard_map/vb,db->vd/dot_general | solution.py:312
  1080.5 39.7 %all-reduce.14 = (f32[1024]{0:T(1024)S(1)}, f32[1024]{0:T(1024)S(1)}) all-reduce(f32[1024]{0:T(1024)S(1)} %get-tuple-element.74, f32[1024]{0:T(1024)S(1)} %get-tuple-element.73), channel_id=1, replica_groups=mesh['col'=4,'ta'=8] {'col','ta'}, use_global_device_ids=true, to_apply=%region_49.50 | all-reduce | flops 2048 | bytes 16384 | tf_op jit(solution)/shard_map/psum | solution.py:38
  1120.2 12.6 multiply_convert_fusion
  1132.8 8.9 fusion.71
  1141.7 40.5 %all-reduce.13 = (f32[256]{0:T(256)S(1)}, f32[256]{0:T(256)S(1)}) all-reduce(f32[256]{0:T(256)S(1)} %get-tuple-element.150, f32[256]{0:T(256)S(1)} %get-tuple-element.149), channel_id=1, replica_groups=mesh['col'=4,'ta'=8] {'col','ta'}, use_global_device_ids=true, to_apply=%region_53.54 | all-reduce | flops 512 | bytes 4096 | tf_op jit(solution)/shard_map/psum | solution.py:38
  1195.4 30.4 %multiply_reduce_fusion.31 = (f32[256]{0:T(256)S(1)}, f32[256]{0:T(256)S(1)}, f32[256]{0:T(256)S(1)}, f32[256]{0:T(256)S(1)}, f32[256]{0:T(256)S(1)}, /*index=5*...) fusion(f32[21,14,14,256]{3,2,1,0:T(8,128)} %reshape.482, ...), kind=kLoop, calls=%fused_computation.123 | loop fusion | flops 37928704 | bytes 14769236 | tf_op jit(solution)/shard_map/reduce_sum | solution.py:88
  1284.8 24.1 %fusion.4 = bf16[21,14,14,256]{3,2,1,0:T(8,128)(2,1)} fusion(f32[20,14,14,256]{3,2,1,0:T(8,128)} %slice.990, f32[1,14,14,256]{3,2,1,0:T(8,128)} %fusion.55, f32[21,14,14,256]{3,2,1,0:T(8,128)S(1)} %fusion.45, f32[21,14,14,256]{3,2,1,0:T(8,128)} %reshape.482, f32[21]{0:T(128)S(1)} %fusion.67, f32[256]{0:T(256)S(1)} %bitcast.262, f32[256]{0:T(256)} %bitcast.264, ...), kind=kLoop, calls=%fused_computation.97 | loop fusion | flops 23181312 | bytes 14761044 | tf_op jit(solution)/shard_map/convert_element_type | solution.py:291
  1318.7 39.9 %all-reduce.12 = (f32[256]{0:T(256)S(1)}, f32[256]{0:T(256)S(1)}, f32[2,27,256]{2,1,0:T(8,128)S(1)}) all-reduce(f32[256]{0:T(256)S(1)} %get-tuple-element.148, f32[256]{0:T(256)S(1)} %get-tuple-element.147, f32[2,27,256]{2,1,0:T(8,128)S(1)} %copy-done.39), channel_id=1, replica_groups=mesh['col'=4,'ta'=8] {'col','ta'}, use_global_device_ids=true, to_apply=%region_57.58 | all-reduce | flops 14336 | bytes 114688 | tf_op jit(solution)/shard_map/psum | solution.py:38
  1371.5 11.5 add_convert_fusion
  1383.0 12.8 convert_element_type.251
  1397.7 14.3 broadcast_select_fusion
  1412.0 105.3 %all-reduce.21.cloned.1.call-done = (f32[2,1024,256]{1,2,0:T(8,128)}, f32[2,256,256]{2,1,0:T(8,128)}, f32[2,256,1024]{2,1,0:T(8,128)}) async-done(((f32[2,1024,256]{1,2,0:T(8,128)}, f32[2,256,256]{2,1,0:T(8,128)}, f32[2,256,1024]{2,1,0:T(8,128)}), (f32[2,1024,256]{1,2,0:T(8,128)}, f32[2,256,256]{2,1,0:T(8,128)}, f32[2,256,1024]{2,1,0:T(8,128)})) %all-reduce.21.cloned.1.call-update) | async-done | bytes 4718608 | tf_op jit(solution)/shard_map/psum | solution.py:329
  (464 shorter events, 330.9 us)
Async XLA Ops:
  7.2 1510.1 %all-reduce.21.cloned.1.call-start = ((), (), s32[]{:S(2)}) async-start(), calls=%async_computation | async-start | bytes 9437184 | tf_op jit(solution)/shard_map/psum | solution.py:329
  22.9 76.2 %copy-start.133 = (bf16[2,2,256]{2,1,0:T(2,128)(2,1)S(1)}, bf16[2,2,256]{2,1,0:T(2,128)(2,1)}, u32[]{:S(2)}) copy-start(bf16[2,2,256]{2,1,0:T(2,128)(2,1)} %param.20) | copy-start | bytes 6148
  22.9 76.2 %copy-start.134 = (bf16[2,2,256]{2,1,0:T(2,128)(2,1)S(1)}, bf16[2,2,256]{2,1,0:T(2,128)(2,1)}, u32[]{:S(2)}) copy-start(bf16[2,2,256]{2,1,0:T(2,128)(2,1)} %param.21) | copy-start | bytes 6148
  58.7 45.6 %copy-start.49 = (f32[256]{0:T(256)}, f32[256]{0:T(256)S(1)}, u32[]{:S(2)}) copy-start(f32[256]{0:T(256)S(1)} %broadcast_multiply_fusion.13) | copy-start | bytes 3076
  58.7 47.0 %copy-start.36 = (bf16[2,256,256]{2,1,0:T(8,128)(2,1)S(1)}, bf16[2,256,256]{2,1,0:T(8,128)(2,1)}, u32[]{:S(2)}) copy-start(bf16[2,256,256]{2,1,0:T(8,128)(2,1)} %param.17) | copy-start | bytes 786436
  99.6 197.3 %copy-start.118 = (f32[1,1,256]{2,1,0:T(1,128)}, f32[1,1,256]{2,1,0:T(1,128)S(1)}, u32[]{:S(2)}) copy-start(f32[1,1,256]{2,1,0:T(1,128)S(1)} %get-tuple-element.302) | copy-start | bytes 3076
  109.5 55.2 %collective-permute-start = (bf16[1,14,14,256]{3,2,1,0:T(8,128)(2,1)S(1)}, bf16[1,14,14,256]{3,2,1,0:T(8,128)(2,1)S(1)}, u32[]{:S(2)}, u32[]{:S(2)}) collective-permute-start(bf16[1,14,14,256]{3,2,1,0:T(8,128)(2,1)S(1)} %constant_dynamic-slice_fusion.4), channel_id=1, source_target_pairs={{0,1},{1,2},{2,3},{3,4},{4,5},{5,6},{6,7},{8,9},{9,10},{10,11},{11... | collective-permute-start | bytes 301064 | tf_op jit(solution)/shard_map/ppermute | solution.py:17
  110.8 50.8 %collective-permute-start.1 = (bf16[1,14,14,256]{3,2,1,0:T(8,128)(2,1)S(1)}, bf16[1,14,14,256]{3,2,1,0:T(8,128)(2,1)S(1)}, u32[]{:S(2)}, u32[]{:S(2)}) collective-permute-start(bf16[1,14,14,256]{3,2,1,0:T(8,128)(2,1)S(1)} %slice.781), channel_id=1, source_target_pairs={{1,0},{2,1},{3,2},{4,3},{5,4},{6,5},{7,6},{9,8},{10,9},{11,10},{12... | collective-permute-start | bytes 301064 | tf_op jit(solution)/shard_map/ppermute | solution.py:18
  116.2 51.5 %copy-start.64 = (f32[1,1,256]{2,0,1:T(1,128)}, f32[1,1,256]{2,0,1:T(1,128)S(1)}, u32[]{:S(2)}) copy-start(f32[1,1,256]{2,0,1:T(1,128)S(1)} %get-tuple-element.229) | copy-start | bytes 3076
  116.2 51.5 %copy-start.66 = (f32[1,1,256]{2,0,1:T(1,128)}, f32[1,1,256]{2,0,1:T(1,128)S(1)}, u32[]{:S(2)}) copy-start(f32[1,1,256]{2,0,1:T(1,128)S(1)} %get-tuple-element.230) | copy-start | bytes 3076
  116.2 51.5 %copy-start.67 = (f32[1,1,256]{2,0,1:T(1,128)}, f32[1,1,256]{2,0,1:T(1,128)S(1)}, u32[]{:S(2)}) copy-start(f32[1,1,256]{2,0,1:T(1,128)S(1)} %get-tuple-element.231) | copy-start | bytes 3076
  116.2 51.5 %copy-start.68 = (f32[1,1,256]{2,0,1:T(1,128)}, f32[1,1,256]{2,0,1:T(1,128)S(1)}, u32[]{:S(2)}) copy-start(f32[1,1,256]{2,0,1:T(1,128)S(1)} %get-tuple-element.232) | copy-start | bytes 3076
  116.2 51.5 %copy-start.69 = (f32[1,1,256]{2,0,1:T(1,128)}, f32[1,1,256]{2,0,1:T(1,128)S(1)}, u32[]{:S(2)}) copy-start(f32[1,1,256]{2,0,1:T(1,128)S(1)} %get-tuple-element.233) | copy-start | bytes 3076
  116.3 51.5 %copy-start.70 = (f32[1,1,256]{2,0,1:T(1,128)}, f32[1,1,256]{2,0,1:T(1,128)S(1)}, u32[]{:S(2)}) copy-start(f32[1,1,256]{2,0,1:T(1,128)S(1)} %get-tuple-element.234) | copy-start | bytes 3076
  116.3 51.5 %copy-start.71 = (f32[1,1,256]{2,0,1:T(1,128)}, f32[1,1,256]{2,0,1:T(1,128)S(1)}, u32[]{:S(2)}) copy-start(f32[1,1,256]{2,0,1:T(1,128)S(1)} %get-tuple-element.235) | copy-start | bytes 3076
  116.3 51.5 %copy-start.72 = (f32[1,1,256]{2,0,1:T(1,128)}, f32[1,1,256]{2,0,1:T(1,128)S(1)}, u32[]{:S(2)}) copy-start(f32[1,1,256]{2,0,1:T(1,128)S(1)} %get-tuple-element.236) | copy-start | bytes 3076
  116.3 51.5 %copy-start.73 = (f32[1,1,256]{2,0,1:T(1,128)}, f32[1,1,256]{2,0,1:T(1,128)S(1)}, u32[]{:S(2)}) copy-start(f32[1,1,256]{2,0,1:T(1,128)S(1)} %get-tuple-element.237) | copy-start | bytes 3076
  116.3 51.5 %copy-start.74 = (f32[1,1,256]{2,0,1:T(1,128)}, f32[1,1,256]{2,0,1:T(1,128)S(1)}, u32[]{:S(2)}) copy-start(f32[1,1,256]{2,0,1:T(1,128)S(1)} %get-tuple-element.220) | copy-start | bytes 3076
  116.3 51.5 %copy-start.76 = (f32[1,1,256]{2,0,1:T(1,128)}, f32[1,1,256]{2,0,1:T(1,128)S(1)}, u32[]{:S(2)}) copy-start(f32[1,1,256]{2,0,1:T(1,128)S(1)} %get-tuple-element.221) | copy-start | bytes 3076
  116.3 51.5 %copy-start.78 = (f32[1,1,256]{2,0,1:T(1,128)}, f32[1,1,256]{2,0,1:T(1,128)S(1)}, u32[]{:S(2)}) copy-start(f32[1,1,256]{2,0,1:T(1,128)S(1)} %get-tuple-element.222) | copy-start | bytes 3076
  116.3 51.5 %copy-start.80 = (f32[1,1,256]{2,0,1:T(1,128)}, f32[1,1,256]{2,0,1:T(1,128)S(1)}, u32[]{:S(2)}) copy-start(f32[1,1,256]{2,0,1:T(1,128)S(1)} %get-tuple-element.223) | copy-start | bytes 3076
  116.3 51.5 %copy-start.82 = (f32[1,1,256]{2,0,1:T(1,128)}, f32[1,1,256]{2,0,1:T(1,128)S(1)}, u32[]{:S(2)}) copy-start(f32[1,1,256]{2,0,1:T(1,128)S(1)} %get-tuple-element.224) | copy-start | bytes 3076
  116.3 51.5 %copy-start.84 = (f32[1,1,256]{2,0,1:T(1,128)}, f32[1,1,256]{2,0,1:T(1,128)S(1)}, u32[]{:S(2)}) copy-start(f32[1,1,256]{2,0,1:T(1,128)S(1)} %get-tuple-element.225) | copy-start | bytes 3076
  116.4 51.5 %copy-start.86 = (f32[1,1,256]{2,0,1:T(1,128)}, f32[1,1,256]{2,0,1:T(1,128)S(1)}, u32[]{:S(2)}) copy-start(f32[1,1,256]{2,0,1:T(1,128)S(1)} %get-tuple-element.226) | copy-start | bytes 3076
  116.4 51.5 %copy-start.88 = (f32[1,1,256]{2,0,1:T(1,128)}, f32[1,1,256]{2,0,1:T(1,128)S(1)}, u32[]{:S(2)}) copy-start(f32[1,1,256]{2,0,1:T(1,128)S(1)} %get-tuple-element.227) | copy-start | bytes 3076
  116.4 51.5 %copy-start.90 = (f32[1,1,256]{2,0,1:T(1,128)}, f32[1,1,256]{2,0,1:T(1,128)S(1)}, u32[]{:S(2)}) copy-start(f32[1,1,256]{2,0,1:T(1,128)S(1)} %get-tuple-element.228) | copy-start | bytes 3076
  116.4 51.5 %copy-start.92 = (f32[1,1,256]{2,0,1:T(1,128)}, f32[1,1,256]{2,0,1:T(1,128)S(1)}, u32[]{:S(2)}) copy-start(f32[1,1,256]{2,0,1:T(1,128)S(1)} %get-tuple-element.219) | copy-start | bytes 3076
  116.4 51.5 %copy-start.94 = (f32[1,1,256]{2,0,1:T(1,128)}, f32[1,1,256]{2,0,1:T(1,128)S(1)}, u32[]{:S(2)}) copy-start(f32[1,1,256]{2,0,1:T(1,128)S(1)} %get-tuple-element.291) | copy-start | bytes 3076
  116.4 51.5 %copy-start.96 = (f32[1,1,256]{2,0,1:T(1,128)}, f32[1,1,256]{2,0,1:T(1,128)S(1)}, u32[]{:S(2)}) copy-start(f32[1,1,256]{2,0,1:T(1,128)S(1)} %get-tuple-element.292) | copy-start | bytes 3076
  116.4 51.5 %copy-start.98 = (f32[1,1,256]{2,0,1:T(1,128)}, f32[1,1,256]{2,0,1:T(1,128)S(1)}, u32[]{:S(2)}) copy-start(f32[1,1,256]{2,0,1:T(1,128)S(1)} %get-tuple-element.293) | copy-start | bytes 3076
  116.4 51.5 %copy-start.100 = (f32[1,1,256]{2,0,1:T(1,128)}, f32[1,1,256]{2,0,1:T(1,128)S(1)}, u32[]{:S(2)}) copy-start(f32[1,1,256]{2,0,1:T(1,128)S(1)} %get-tuple-element.294) | copy-start | bytes 3076
  116.5 51.5 %copy-start.102 = (f32[1,1,256]{2,0,1:T(1,128)}, f32[1,1,256]{2,0,1:T(1,128)S(1)}, u32[]{:S(2)}) copy-start(f32[1,1,256]{2,0,1:T(1,128)S(1)} %get-tuple-element.295) | copy-start | bytes 3076
  116.5 51.5 %copy-start.104 = (f32[1,1,256]{2,0,1:T(1,128)}, f32[1,1,256]{2,0,1:T(1,128)S(1)}, u32[]{:S(2)}) copy-start(f32[1,1,256]{2,0,1:T(1,128)S(1)} %get-tuple-element.296) | copy-start | bytes 3076
  116.5 51.5 %copy-start.106 = (f32[1,1,256]{2,0,1:T(1,128)}, f32[1,1,256]{2,0,1:T(1,128)S(1)}, u32[]{:S(2)}) copy-start(f32[1,1,256]{2,0,1:T(1,128)S(1)} %get-tuple-element.297) | copy-start | bytes 3076
  116.5 51.5 %copy-start.108 = (f32[1,1,256]{2,0,1:T(1,128)}, f32[1,1,256]{2,0,1:T(1,128)S(1)}, u32[]{:S(2)}) copy-start(f32[1,1,256]{2,0,1:T(1,128)S(1)} %get-tuple-element.298) | copy-start | bytes 3076
  117.6 264.3 %copy-start.45 = (f32[1,1024]{1,0:T(1,128)}, f32[1,1024]{1,0:T(1,128)S(1)}, u32[]{:S(2)}) copy-start(f32[1,1024]{1,0:T(1,128)S(1)} %get-tuple-element.251) | copy-start | bytes 12292
  117.7 264.3 %copy-start.55 = (f32[1,1024]{1,0:T(1,128)}, f32[1,1024]{1,0:T(1,128)S(1)}, u32[]{:S(2)}) copy-start(f32[1,1024]{1,0:T(1,128)S(1)} %get-tuple-element.253) | copy-start | bytes 12292
  491.0 19.6 %collective-permute-start.2 = (bf16[1,14,14,256]{3,2,1,0:T(8,128)(2,1)S(1)}, bf16[1,14,14,256]{3,2,1,0:T(8,128)(2,1)S(1)}, u32[]{:S(2)}, u32[]{:S(2)}) collective-permute-start(bf16[1,14,14,256]{3,2,1,0:T(8,128)(2,1)S(1)} %constant_dynamic-slice_fusion.3), channel_id=1, source_target_pairs={{0,1},{1,2},{2,3},{3,4},{4,5},{5,6},{6,7},{8,9},{9,10},{10,11},{11... | collective-permute-start | bytes 301064 | tf_op jit(solution)/shard_map/ppermute | solution.py:17
  492.3 15.3 collective-permute-start.3
  810.8 48.4 %copy-start.12 = (bf16[20,14,14,256]{3,2,1,0:T(8,128)(2,1)S(1)}, bf16[20,14,14,256]{3,2,1,0:T(8,128)(2,1)}, u32[]{:S(2)}) copy-start(bf16[20,14,14,256]{3,2,1,0:T(8,128)(2,1)} %slice.812) | copy-start | bytes 6021124
  939.4 38.6 %collective-permute-start.5 = (bf16[1,14,14,256]{3,2,1,0:T(8,128)(2,1)S(1)}, bf16[1,14,14,256]{3,2,1,0:T(8,128)(2,1)S(1)}, u32[]{:S(2)}, u32[]{:S(2)}) collective-permute-start(bf16[1,14,14,256]{3,2,1,0:T(8,128)(2,1)S(1)} %slice.1406), channel_id=1, source_target_pairs={{1,0},{2,1},{3,2},{4,3},{5,4},{6,5},{7,6},{9,8},{10,9},{11,10},{12... | collective-permute-start | bytes 301064 | tf_op jit(solution)/shard_map/ppermute | solution.py:18
  941.6 36.3 %collective-permute-start.4 = (bf16[1,14,14,256]{3,2,1,0:T(8,128)(2,1)S(1)}, bf16[1,14,14,256]{3,2,1,0:T(8,128)(2,1)S(1)}, u32[]{:S(2)}, u32[]{:S(2)}) collective-permute-start(bf16[1,14,14,256]{3,2,1,0:T(8,128)(2,1)S(1)} %dynamic-slice_convert_fusion.1), channel_id=1, source_target_pairs={{0,1},{1,2},{2,3},{3,4},{4,5},{5,6},{6,7},{8,9},{9,10},{10,11},{11... | collective-permute-start | bytes 301064 | tf_op jit(solution)/shard_map/ppermute | solution.py:17
  1005.5 47.7 %copy-start.123 = (f32[256]{0:T(256)S(1)}, f32[256]{0:T(256)}, u32[]{:S(2)}) copy-start(f32[256]{0:T(256)} %get-tuple-element.270) | copy-start | bytes 3076
  1057.8 62.3 %copy-start.61 = (f32[1024]{0:T(1024)S(1)}, f32[1024]{0:T(1024)}, u32[]{:S(2)}) copy-start(f32[1024]{0:T(1024)} %get-tuple-element.246) | copy-start | bytes 12292
  1132.8 49.9 %copy-start.4 = (bf16[4116,256]{1,0:T(8,128)(2,1)S(1)}, bf16[4116,256]{1,0:T(8,128)(2,1)}, u32[]{:S(2)}) copy-start(bf16[4116,256]{1,0:T(8,128)(2,1)} %copy-done.3) | copy-start | bytes 6322180
  1132.8 49.9 %copy-start.121 = (f32[256]{0:T(256)S(1)}, f32[256]{0:T(256)}, u32[]{:S(2)}) copy-start(f32[256]{0:T(256)} %get-tuple-element.268) | copy-start | bytes 3076
  1270.3 11.9 collective-permute-start.7
  1271.7 10.5 collective-permute-start.6
  (111 other events, 1275.3 us)
Sparse Core Ops, SparseCore 0:
  1371.6 145.6 all-reduce.20
